TPU v7x, 32 devices: a whole 2x2x4 slice. The times are simulated.
32 devices in a mesh: chan: 8 (over y, x, core), cross: 4 (over z).
Axes of the slice: x: 2, y: 2, z: 4, core: 2. Of those that a mesh axis runs over, the one named last changes fastest.
Arguments:
- positions: float32 [2, 32, 64, 128], P(None, 'chan', 'cross'), may hold values from 0 to 1
- velocity: float32 [2, 32, 64, 128], P(None, 'chan', 'cross'), may hold values from -4 to 4
- density: float32 [32, 64, 128], P('chan', 'cross'), may hold values from 0.8 to 1.2
- counts: int32 [32, 64], P('chan', 'cross'), may hold values from 0 to 128, as said below
Outputs:
- new_fields: float32 [5, 32, 64, 128], P(None, 'chan', 'cross')
- lowest_density: float32 [], replicated
Inputs may be any that keep to these rules, and one draw needn't show every extreme that they name: `counts`: in every channel column the bins from cross index 0 up to some height hold particles and those above are empty; the height is 56 or more; the bins at cross index 0 hold 128 particles.
All inputs are finite; a program needn't handle non-finite values.
Results may differ from a plain program's by a relative error of at most 0.0001.
Values sent between devices are 32-bit elements; how exact they have to be, the bound alone decides.
A program may use at most 64 MiB of HBM per device.

v0:
```python
import math

import jax
import jax.numpy as jnp
from jax import lax
from jax.sharding import PartitionSpec as P

FAR_SHIFT = 8.0
SOUND_SQ = 100.0
KERNEL_GRAD = 140.0 / math.pi
PARTICLE_MASS = 1.0 / 128.0
GRAVITY = 1.0
TIME_STEP = 0.025


def padded_2(x, sides, width):
    for axis, dim in sides:
        size, length = (lax.axis_size(axis), x.shape[dim])
        up = [(i, (i + 1) % size) for i in range(size)]
        down = [(j, i) for i, j in up]
        last = lax.slice_in_dim(x, length - width, length, axis=dim)
        leading = lax.slice_in_dim(x, 0, width, axis=dim)
        before = lax.ppermute(last, axis, up)
        after = lax.ppermute(leading, axis, down)
        x = jnp.concatenate([before, x, after], axis=dim)
    return x


def pack_fields(positions, velocity, density, occupied):
    return jnp.stack(
        [
            (positions[0] + FAR_SHIFT) * occupied,
            (positions[1] + FAR_SHIFT) * occupied,
            velocity[0] * occupied,
            velocity[1] * occupied,
            density * occupied,
        ]
    )


def column_rates(window):
    bin_rows = window.shape[2] - 2
    centre = window[:, 1, 1 : bin_rows + 1]
    centre_pressure = SOUND_SQ * (centre[4] - 1.0)
    force_x = jnp.zeros_like(centre[0])
    force_y = jnp.zeros_like(centre[0])
    compress = jnp.zeros_like(centre[0])
    for offset_col in (-1, 0, 1):
        for offset_row in (-1, 0, 1):
            neighbour = window[:, 1 + offset_col, 1 + offset_row : 1 + offset_row + bin_rows]
            delta_x = centre[0][:, :, None] - neighbour[0][:, None, :] - offset_col
            delta_y = centre[1][:, :, None] - neighbour[1][:, None, :] - offset_row
            radius = jnp.sqrt(delta_x * delta_x + delta_y * delta_y)
            weight = jnp.maximum(1.0 - radius, 0.0) ** 3
            pressure = (
                centre_pressure[:, :, None] + SOUND_SQ * (neighbour[4][:, None, :] - 1.0)
            ) * weight
            force_x = force_x + jnp.sum(pressure * delta_x, axis=2)
            force_y = force_y + jnp.sum(pressure * delta_y, axis=2)
            closing = (centre[2][:, :, None] - neighbour[2][:, None, :]) * delta_x + (
                centre[3][:, :, None] - neighbour[3][:, None, :]
            ) * delta_y
            compress = compress + jnp.sum(weight * closing, axis=2)
    force_scale = KERNEL_GRAD * PARTICLE_MASS
    return jnp.stack(
        [force_scale * force_x, force_scale * force_y - GRAVITY, -force_scale * compress]
    )


def extend_rims(fields):
    extended = padded_2(fields, (("chan", 1), ("cross", 2)), 1)
    cross_place = lax.axis_index("cross")
    cross_count = lax.axis_size("cross")
    rim_row = jnp.arange(extended.shape[2], dtype=jnp.int32)
    lower_open = jnp.logical_or(rim_row != 0, cross_place > 0)
    upper_open = jnp.logical_or(rim_row != extended.shape[2] - 1, cross_place < cross_count - 1)
    wall_keep = jnp.logical_and(lower_open, upper_open).astype(jnp.float32)
    extended = extended * wall_keep[None, None, :, None]
    return extended


def local_rates(fields):
    padded = extend_rims(fields)
    columns = jnp.arange(fields.shape[1], dtype=jnp.int32)

    def one_column(column):
        return column_rates(lax.dynamic_slice_in_dim(padded, column, 3, 1))

    per_column = lax.map(one_column, columns)
    return jnp.transpose(per_column, (1, 0, 2, 3))


def body(positions, velocity, density, counts):
    slot_index = jnp.arange(positions.shape[-1], dtype=jnp.int32)
    occupied = (slot_index[None, None, :] < counts[:, :, None]).astype(jnp.float32)
    fields = pack_fields(positions, velocity, density, occupied)
    first_rates = local_rates(fields)
    half_step = 0.5 * TIME_STEP
    predicted = (
        jnp.stack(
            [
                fields[0] + half_step * fields[2],
                fields[1] + half_step * fields[3],
                fields[2] + half_step * first_rates[0],
                fields[3] + half_step * first_rates[1],
                fields[4] + half_step * first_rates[2],
            ]
        )
        * occupied
    )
    second_rates = local_rates(predicted)
    final_ux = fields[2] + TIME_STEP * second_rates[0]
    final_uy = fields[3] + TIME_STEP * second_rates[1]
    final_x = fields[0] + half_step * (fields[2] + final_ux) - FAR_SHIFT
    final_y = fields[1] + half_step * (fields[3] + final_uy) - FAR_SHIFT
    final_density = fields[4] + TIME_STEP * second_rates[2]
    new_fields = jnp.stack([final_x, final_y, final_ux, final_uy, final_density]) * occupied
    own_lowest = jnp.min(jnp.where(occupied > 0.0, final_density, 1000000000.0))
    lowest = lax.pmin(own_lowest, ("chan", "cross"))
    return (new_fields, lowest)


def solution(mesh):
    return jax.shard_map(
        body,
        mesh=mesh,
        in_specs=(
            P(None, "chan", "cross", None),
            P(None, "chan", "cross", None),
            P("chan", "cross", None),
            P("chan", "cross"),
        ),
        out_specs=(P(None, "chan", "cross", None), P()),
        check_vma=False,
    )
```

profile of v0, /device:TPU:0, one launch (start us, length us, event | category | flops | bytes accessed | tf_op | source)
XLA Modules:
  0.0 241.1 jit_solution(17284415380711107578)
XLA Ops:
  0.7 0.9 constant_dynamic-update-slice_fusion.4
  1.8 0.7 copy-done.2
  2.6 0.5 collective-permute-start
  3.1 2.9 %collective-permute-start.1 = (f32[5,1,16,128]{3,2,1,0:T(8,128)S(1)}, f32[5,1,16,128]{3,2,1,0:T(8,128)S(1)}, u32[]{:S(2)}, u32[]{:S(2)}) collective-permute-start(f32[5,1,16,128]{3,2,1,0:T(8,128)S(1)} %get-tuple-element.375), channel_id=1, source_target_pairs={{4,0},{8,4},{12,8},{16,12},{20,16},{24,20},{28,24},{0,28},{5,1},{9... | collective-permute-start | bytes 122888 | tf_op jit(solution)/shard_map/ppermute | solution.py:24
  6.1 1.5 collective-permute-done
  7.7 2.3 collective-permute-start.2
  10.1 2.1 collective-permute-start.3
  12.2 1.9 collective-permute-done.2
  14.3 87.6 %while.26 = (s32[]{:T(128)}, f32[4,3,16,128]{3,2,0,1:T(8,128)S(1)}, s32[4]{0:T(128)S(1)}, f32[5,6,18,128]{3,2,1,0:T(8,128)S(1)}, s32[]{:T(128)}, /*index=5*/s32[...) while((s32[]{:T(128)}, f32[4,3,16,128]{3,2,0,1:T(8,128)S(1)}, s32[4]{0:T(128)S(1)}, ...), condition=%wide.region_28.29_spmd, body=%wide.region_0.28_spmd.sunk | while | flops 60606472 | bytes 1761539 | solution.py:89
  14.3 0.6 dynamic_slice.31
  16.8 0.2 fusion.230
  17.0 5.4 %multiply_reduce_fusion.43 = (f32[16,128]{1,0:T(8,128)S(1)}, f32[16,128]{1,0:T(8,128)S(1)}, f32[16,128]{1,0:T(8,128)S(1)}, f32[16,128]{1,0:T(8,128)S(1)}, f32[16...) fusion(f32[16,128]{1,0:T(8,128)S(1)} %get-tuple-element.611, ...), kind=kLoop, calls=%fused_computation.94.clone.1 | loop fusion | flops 16498688 | bytes 212992 | tf_op jit(solution)/shard_map/while/body/eval_jaxpr/reduce_sum | solution.py:58
  22.4 5.3 %multiply_reduce_fusion.42 = (f32[16,128]{1,0:T(8,128)S(1)}, f32[16,128]{1,0:T(8,128)S(1)}, f32[16,128]{1,0:T(8,128)S(1)}, f32[16,128]{1,0:T(8,128)S(1)}, f32[16...) fusion(f32[16,128]{1,0:T(8,128)S(1)} %get-tuple-element.596, ...), kind=kLoop, calls=%fused_computation.101.clone.1 | loop fusion | flops 17025024 | bytes 212992 | tf_op jit(solution)/shard_map/while/body/eval_jaxpr/reduce_sum | solution.py:58
  27.8 6.7 %multiply_reduce_fusion.41 = (f32[16,128]{1,0:T(8,128)S(1)}, f32[16,128]{1,0:T(8,128)S(1)}, f32[16,128]{1,0:T(8,128)S(1)}, f32[16,128]{1,0:T(8,128)S(1)}, f32[16...) fusion(f32[16,128]{1,0:T(8,128)S(1)} %get-tuple-element.581, ...), kind=kLoop, calls=%fused_computation.98.clone.1 | loop fusion | flops 22523904 | bytes 237568 | tf_op jit(solution)/shard_map/while/body/eval_jaxpr/reduce_sum | solution.py:58
  34.5 1.6 multiply_reduce_fusion.40
  36.2 0.6 dynamic_slice.31
  38.7 0.2 fusion.230
  38.9 5.4 %multiply_reduce_fusion.43 = (f32[16,128]{1,0:T(8,128)S(1)}, f32[16,128]{1,0:T(8,128)S(1)}, f32[16,128]{1,0:T(8,128)S(1)}, f32[16,128]{1,0:T(8,128)S(1)}, f32[16...) fusion(f32[16,128]{1,0:T(8,128)S(1)} %get-tuple-element.611, ...), kind=kLoop, calls=%fused_computation.94.clone.1 | loop fusion | flops 16498688 | bytes 212992 | tf_op jit(solution)/shard_map/while/body/eval_jaxpr/reduce_sum | solution.py:58
  44.3 5.3 %multiply_reduce_fusion.42 = (f32[16,128]{1,0:T(8,128)S(1)}, f32[16,128]{1,0:T(8,128)S(1)}, f32[16,128]{1,0:T(8,128)S(1)}, f32[16,128]{1,0:T(8,128)S(1)}, f32[16...) fusion(f32[16,128]{1,0:T(8,128)S(1)} %get-tuple-element.596, ...), kind=kLoop, calls=%fused_computation.101.clone.1 | loop fusion | flops 17025024 | bytes 212992 | tf_op jit(solution)/shard_map/while/body/eval_jaxpr/reduce_sum | solution.py:58
  49.6 6.7 %multiply_reduce_fusion.41 = (f32[16,128]{1,0:T(8,128)S(1)}, f32[16,128]{1,0:T(8,128)S(1)}, f32[16,128]{1,0:T(8,128)S(1)}, f32[16,128]{1,0:T(8,128)S(1)}, f32[16...) fusion(f32[16,128]{1,0:T(8,128)S(1)} %get-tuple-element.581, ...), kind=kLoop, calls=%fused_computation.98.clone.1 | loop fusion | flops 22523904 | bytes 237568 | tf_op jit(solution)/shard_map/while/body/eval_jaxpr/reduce_sum | solution.py:58
  56.3 1.6 multiply_reduce_fusion.40
  58.0 0.6 dynamic_slice.31
  60.6 0.2 fusion.230
  60.8 5.4 %multiply_reduce_fusion.43 = (f32[16,128]{1,0:T(8,128)S(1)}, f32[16,128]{1,0:T(8,128)S(1)}, f32[16,128]{1,0:T(8,128)S(1)}, f32[16,128]{1,0:T(8,128)S(1)}, f32[16...) fusion(f32[16,128]{1,0:T(8,128)S(1)} %get-tuple-element.611, ...), kind=kLoop, calls=%fused_computation.94.clone.1 | loop fusion | flops 16498688 | bytes 212992 | tf_op jit(solution)/shard_map/while/body/eval_jaxpr/reduce_sum | solution.py:58
  66.2 5.3 %multiply_reduce_fusion.42 = (f32[16,128]{1,0:T(8,128)S(1)}, f32[16,128]{1,0:T(8,128)S(1)}, f32[16,128]{1,0:T(8,128)S(1)}, f32[16,128]{1,0:T(8,128)S(1)}, f32[16...) fusion(f32[16,128]{1,0:T(8,128)S(1)} %get-tuple-element.596, ...), kind=kLoop, calls=%fused_computation.101.clone.1 | loop fusion | flops 17025024 | bytes 212992 | tf_op jit(solution)/shard_map/while/body/eval_jaxpr/reduce_sum | solution.py:58
  71.5 6.7 %multiply_reduce_fusion.41 = (f32[16,128]{1,0:T(8,128)S(1)}, f32[16,128]{1,0:T(8,128)S(1)}, f32[16,128]{1,0:T(8,128)S(1)}, f32[16,128]{1,0:T(8,128)S(1)}, f32[16...) fusion(f32[16,128]{1,0:T(8,128)S(1)} %get-tuple-element.581, ...), kind=kLoop, calls=%fused_computation.98.clone.1 | loop fusion | flops 22523904 | bytes 237568 | tf_op jit(solution)/shard_map/while/body/eval_jaxpr/reduce_sum | solution.py:58
  78.2 1.6 multiply_reduce_fusion.40
  79.9 0.6 dynamic_slice.31
  82.5 0.2 fusion.230
  82.7 5.4 %multiply_reduce_fusion.43 = (f32[16,128]{1,0:T(8,128)S(1)}, f32[16,128]{1,0:T(8,128)S(1)}, f32[16,128]{1,0:T(8,128)S(1)}, f32[16,128]{1,0:T(8,128)S(1)}, f32[16...) fusion(f32[16,128]{1,0:T(8,128)S(1)} %get-tuple-element.611, ...), kind=kLoop, calls=%fused_computation.94.clone.1 | loop fusion | flops 16498688 | bytes 212992 | tf_op jit(solution)/shard_map/while/body/eval_jaxpr/reduce_sum | solution.py:58
  88.1 5.3 %multiply_reduce_fusion.42 = (f32[16,128]{1,0:T(8,128)S(1)}, f32[16,128]{1,0:T(8,128)S(1)}, f32[16,128]{1,0:T(8,128)S(1)}, f32[16,128]{1,0:T(8,128)S(1)}, f32[16...) fusion(f32[16,128]{1,0:T(8,128)S(1)} %get-tuple-element.596, ...), kind=kLoop, calls=%fused_computation.101.clone.1 | loop fusion | flops 17025024 | bytes 212992 | tf_op jit(solution)/shard_map/while/body/eval_jaxpr/reduce_sum | solution.py:58
  93.4 6.7 %multiply_reduce_fusion.41 = (f32[16,128]{1,0:T(8,128)S(1)}, f32[16,128]{1,0:T(8,128)S(1)}, f32[16,128]{1,0:T(8,128)S(1)}, f32[16,128]{1,0:T(8,128)S(1)}, f32[16...) fusion(f32[16,128]{1,0:T(8,128)S(1)} %get-tuple-element.581, ...), kind=kLoop, calls=%fused_computation.98.clone.1 | loop fusion | flops 22523904 | bytes 237568 | tf_op jit(solution)/shard_map/while/body/eval_jaxpr/reduce_sum | solution.py:58
  100.1 1.6 multiply_reduce_fusion.40
  102.2 2.6 %collective-permute-start.5 = (f32[5,1,16,128]{3,2,1,0:T(8,128)S(1)}, f32[5,1,16,128]{3,2,1,0:T(8,128)S(1)}, u32[]{:S(2)}, u32[]{:S(2)}) collective-permute-start(f32[5,1,16,128]{3,2,1,0:T(8,128)S(1)} %get-tuple-element.373), channel_id=1, source_target_pairs={{4,0},{8,4},{12,8},{16,12},{20,16},{24,20},{28,24},{0,28},{5,1},{9... | collective-permute-start | bytes 122888 | tf_op jit(solution)/shard_map/ppermute | solution.py:24
  104.8 1.7 collective-permute-done.4
  106.5 1.3 collective-permute-start.6
  107.8 2.6 %collective-permute-start.7 = (f32[5,6,1,128]{3,2,1,0:T(1,128)S(1)}, f32[5,6,1,128]{3,2,1,0:T(1,128)S(1)}, u32[]{:S(2)}, u32[]{:S(2)}) collective-permute-start(f32[5,6,1,128]{3,2,1,0:T(1,128)S(1)} %get-tuple-element.369), channel_id=1, source_target_pairs={{1,0},{2,1},{3,2},{0,3},{5,4},{6,5},{7,6},{4,7},{9,8},{10,9},{11,1... | collective-permute-start | bytes 46088 | tf_op jit(solution)/shard_map/ppermute | solution.py:24
  110.4 1.7 collective-permute-done.6
  112.2 87.6 %while.27 = (s32[]{:T(128)}, f32[4,3,16,128]{3,2,0,1:T(8,128)S(1)}, s32[4]{0:T(128)S(1)}, f32[5,6,18,128]{3,2,1,0:T(8,128)S(1)}, s32[]{:T(128)}, /*index=5*/s32[...) while((s32[]{:T(128)}, f32[4,3,16,128]{3,2,0,1:T(8,128)S(1)}, s32[4]{0:T(128)S(1)}, ...), condition=%wide.region_57.58_spmd, body=%wide.region_29.57_spmd.sunk | while | flops 60606472 | bytes 1761539 | solution.py:89
  112.2 0.6 dynamic_slice.32
  114.8 0.2 fusion.232
  115.0 5.4 %multiply_reduce_fusion.47 = (f32[16,128]{1,0:T(8,128)S(1)}, f32[16,128]{1,0:T(8,128)S(1)}, f32[16,128]{1,0:T(8,128)S(1)}, f32[16,128]{1,0:T(8,128)S(1)}, f32[16...) fusion(f32[16,128]{1,0:T(8,128)S(1)} %get-tuple-element.689, ...), kind=kLoop, calls=%fused_computation.312.clone.1 | loop fusion | flops 16498688 | bytes 212992 | tf_op jit(solution)/shard_map/while/body/eval_jaxpr/reduce_sum | solution.py:58
  120.4 5.3 %multiply_reduce_fusion.46 = (f32[16,128]{1,0:T(8,128)S(1)}, f32[16,128]{1,0:T(8,128)S(1)}, f32[16,128]{1,0:T(8,128)S(1)}, f32[16,128]{1,0:T(8,128)S(1)}, f32[16...) fusion(f32[16,128]{1,0:T(8,128)S(1)} %get-tuple-element.674, ...), kind=kLoop, calls=%fused_computation.319.clone.1 | loop fusion | flops 17025024 | bytes 212992 | tf_op jit(solution)/shard_map/while/body/eval_jaxpr/reduce_sum | solution.py:58
  125.7 6.7 %multiply_reduce_fusion.45 = (f32[16,128]{1,0:T(8,128)S(1)}, f32[16,128]{1,0:T(8,128)S(1)}, f32[16,128]{1,0:T(8,128)S(1)}, f32[16,128]{1,0:T(8,128)S(1)}, f32[16...) fusion(f32[16,128]{1,0:T(8,128)S(1)} %get-tuple-element.659, ...), kind=kLoop, calls=%fused_computation.316.clone.1 | loop fusion | flops 22523904 | bytes 237568 | tf_op jit(solution)/shard_map/while/body/eval_jaxpr/reduce_sum | solution.py:58
  132.4 1.6 multiply_reduce_fusion.44
  134.1 0.6 dynamic_slice.32
  136.6 0.2 fusion.232
  136.9 5.4 %multiply_reduce_fusion.47 = (f32[16,128]{1,0:T(8,128)S(1)}, f32[16,128]{1,0:T(8,128)S(1)}, f32[16,128]{1,0:T(8,128)S(1)}, f32[16,128]{1,0:T(8,128)S(1)}, f32[16...) fusion(f32[16,128]{1,0:T(8,128)S(1)} %get-tuple-element.689, ...), kind=kLoop, calls=%fused_computation.312.clone.1 | loop fusion | flops 16498688 | bytes 212992 | tf_op jit(solution)/shard_map/while/body/eval_jaxpr/reduce_sum | solution.py:58
  142.3 5.3 %multiply_reduce_fusion.46 = (f32[16,128]{1,0:T(8,128)S(1)}, f32[16,128]{1,0:T(8,128)S(1)}, f32[16,128]{1,0:T(8,128)S(1)}, f32[16,128]{1,0:T(8,128)S(1)}, f32[16...) fusion(f32[16,128]{1,0:T(8,128)S(1)} %get-tuple-element.674, ...), kind=kLoop, calls=%fused_computation.319.clone.1 | loop fusion | flops 17025024 | bytes 212992 | tf_op jit(solution)/shard_map/while/body/eval_jaxpr/reduce_sum | solution.py:58
  147.6 6.7 %multiply_reduce_fusion.45 = (f32[16,128]{1,0:T(8,128)S(1)}, f32[16,128]{1,0:T(8,128)S(1)}, f32[16,128]{1,0:T(8,128)S(1)}, f32[16,128]{1,0:T(8,128)S(1)}, f32[16...) fusion(f32[16,128]{1,0:T(8,128)S(1)} %get-tuple-element.659, ...), kind=kLoop, calls=%fused_computation.316.clone.1 | loop fusion | flops 22523904 | bytes 237568 | tf_op jit(solution)/shard_map/while/body/eval_jaxpr/reduce_sum | solution.py:58
  154.3 1.6 multiply_reduce_fusion.44
  156.0 0.6 dynamic_slice.32
  158.8 5.4 %multiply_reduce_fusion.47 = (f32[16,128]{1,0:T(8,128)S(1)}, f32[16,128]{1,0:T(8,128)S(1)}, f32[16,128]{1,0:T(8,128)S(1)}, f32[16,128]{1,0:T(8,128)S(1)}, f32[16...) fusion(f32[16,128]{1,0:T(8,128)S(1)} %get-tuple-element.689, ...), kind=kLoop, calls=%fused_computation.312.clone.1 | loop fusion | flops 16498688 | bytes 212992 | tf_op jit(solution)/shard_map/while/body/eval_jaxpr/reduce_sum | solution.py:58
  164.2 5.3 %multiply_reduce_fusion.46 = (f32[16,128]{1,0:T(8,128)S(1)}, f32[16,128]{1,0:T(8,128)S(1)}, f32[16,128]{1,0:T(8,128)S(1)}, f32[16,128]{1,0:T(8,128)S(1)}, f32[16...) fusion(f32[16,128]{1,0:T(8,128)S(1)} %get-tuple-element.674, ...), kind=kLoop, calls=%fused_computation.319.clone.1 | loop fusion | flops 17025024 | bytes 212992 | tf_op jit(solution)/shard_map/while/body/eval_jaxpr/reduce_sum | solution.py:58
  169.5 6.7 %multiply_reduce_fusion.45 = (f32[16,128]{1,0:T(8,128)S(1)}, f32[16,128]{1,0:T(8,128)S(1)}, f32[16,128]{1,0:T(8,128)S(1)}, f32[16,128]{1,0:T(8,128)S(1)}, f32[16...) fusion(f32[16,128]{1,0:T(8,128)S(1)} %get-tuple-element.659, ...), kind=kLoop, calls=%fused_computation.316.clone.1 | loop fusion | flops 22523904 | bytes 237568 | tf_op jit(solution)/shard_map/while/body/eval_jaxpr/reduce_sum | solution.py:58
  176.2 1.6 multiply_reduce_fusion.44
  177.9 0.6 dynamic_slice.32
  180.6 5.4 %multiply_reduce_fusion.47 = (f32[16,128]{1,0:T(8,128)S(1)}, f32[16,128]{1,0:T(8,128)S(1)}, f32[16,128]{1,0:T(8,128)S(1)}, f32[16,128]{1,0:T(8,128)S(1)}, f32[16...) fusion(f32[16,128]{1,0:T(8,128)S(1)} %get-tuple-element.689, ...), kind=kLoop, calls=%fused_computation.312.clone.1 | loop fusion | flops 16498688 | bytes 212992 | tf_op jit(solution)/shard_map/while/body/eval_jaxpr/reduce_sum | solution.py:58
  186.1 5.3 %multiply_reduce_fusion.46 = (f32[16,128]{1,0:T(8,128)S(1)}, f32[16,128]{1,0:T(8,128)S(1)}, f32[16,128]{1,0:T(8,128)S(1)}, f32[16,128]{1,0:T(8,128)S(1)}, f32[16...) fusion(f32[16,128]{1,0:T(8,128)S(1)} %get-tuple-element.674, ...), kind=kLoop, calls=%fused_computation.319.clone.1 | loop fusion | flops 17025024 | bytes 212992 | tf_op jit(solution)/shard_map/while/body/eval_jaxpr/reduce_sum | solution.py:58
  191.4 6.7 %multiply_reduce_fusion.45 = (f32[16,128]{1,0:T(8,128)S(1)}, f32[16,128]{1,0:T(8,128)S(1)}, f32[16,128]{1,0:T(8,128)S(1)}, f32[16,128]{1,0:T(8,128)S(1)}, f32[16...) fusion(f32[16,128]{1,0:T(8,128)S(1)} %get-tuple-element.659, ...), kind=kLoop, calls=%fused_computation.316.clone.1 | loop fusion | flops 22523904 | bytes 237568 | tf_op jit(solution)/shard_map/while/body/eval_jaxpr/reduce_sum | solution.py:58
  198.1 1.6 multiply_reduce_fusion.44
  199.9 0.7 select_reduce_fusion
  200.9 0.7 broadcast_multiply_fusion
  201.5 39.5 %pmin.7 = f32[]{:T(128)} all-reduce(f32[]{:T(128)} %select_reduce_fusion), channel_id=1, replica_groups=mesh['chan'=8,'cross'=4] {'chan','cross'}, use_global_device_ids=true, to_apply=%region_59.60 | all-reduce | flops 1 | bytes 8 | tf_op jit(solution)/shard_map/pmin | solution.py:119
  (63 shorter events, 2.3 us)
Async XLA Ops:
  0.6 0.9 copy-start.3
  0.6 0.9 copy-start.1
  0.6 1.0 copy-start
  1.7 0.8 copy-start.2
  2.6 5.1 %collective-permute-start = (f32[5,1,16,128]{3,2,1,0:T(8,128)S(1)}, f32[5,1,16,128]{3,2,1,0:T(8,128)S(1)}, u32[]{:S(2)}, u32[]{:S(2)}) collective-permute-start(f32[5,1,16,128]{3,2,1,0:T(8,128)S(1)} %get-tuple-element.374), channel_id=1, source_target_pairs={{0,4},{4,8},{8,12},{12,16},{16,20},{20,24},{24,28},{28,0},{1,5},{5... | collective-permute-start | bytes 122888 | tf_op jit(solution)/shard_map/ppermute | solution.py:23
  3.1 4.6 %collective-permute-start.1 = (f32[5,1,16,128]{3,2,1,0:T(8,128)S(1)}, f32[5,1,16,128]{3,2,1,0:T(8,128)S(1)}, u32[]{:S(2)}, u32[]{:S(2)}) collective-permute-start(f32[5,1,16,128]{3,2,1,0:T(8,128)S(1)} %get-tuple-element.375), channel_id=1, source_target_pairs={{4,0},{8,4},{12,8},{16,12},{20,16},{24,20},{28,24},{0,28},{5,1},{9... | collective-permute-start | bytes 122888 | tf_op jit(solution)/shard_map/ppermute | solution.py:24
  7.7 6.3 %collective-permute-start.2 = (f32[5,6,1,128]{3,2,1,0:T(1,128)S(1)}, f32[5,6,1,128]{3,2,1,0:T(1,128)S(1)}, u32[]{:S(2)}, u32[]{:S(2)}) collective-permute-start(f32[5,6,1,128]{3,2,1,0:T(1,128)S(1)} %get-tuple-element.370), channel_id=1, source_target_pairs={{0,1},{1,2},{2,3},{3,0},{4,5},{5,6},{6,7},{7,4},{8,9},{9,10},{10,1... | collective-permute-start | bytes 46088 | tf_op jit(solution)/shard_map/ppermute | solution.py:23
  10.1 4.1 %collective-permute-start.3 = (f32[5,6,1,128]{3,2,1,0:T(1,128)S(1)}, f32[5,6,1,128]{3,2,1,0:T(1,128)S(1)}, u32[]{:S(2)}, u32[]{:S(2)}) collective-permute-start(f32[5,6,1,128]{3,2,1,0:T(1,128)S(1)} %get-tuple-element.371), channel_id=1, source_target_pairs={{1,0},{2,1},{3,2},{0,3},{5,4},{6,5},{7,6},{4,7},{9,8},{10,9},{11,1... | collective-permute-start | bytes 46088 | tf_op jit(solution)/shard_map/ppermute | solution.py:24
  102.1 4.4 %collective-permute-start.4 = (f32[5,1,16,128]{3,2,1,0:T(8,128)S(1)}, f32[5,1,16,128]{3,2,1,0:T(8,128)S(1)}, u32[]{:S(2)}, u32[]{:S(2)}) collective-permute-start(f32[5,1,16,128]{3,2,1,0:T(8,128)S(1)} %get-tuple-element.372), channel_id=1, source_target_pairs={{0,4},{4,8},{8,12},{12,16},{16,20},{20,24},{24,28},{28,0},{1,5},{5... | collective-permute-start | bytes 122888 | tf_op jit(solution)/shard_map/ppermute | solution.py:23
  102.2 4.3 %collective-permute-start.5 = (f32[5,1,16,128]{3,2,1,0:T(8,128)S(1)}, f32[5,1,16,128]{3,2,1,0:T(8,128)S(1)}, u32[]{:S(2)}, u32[]{:S(2)}) collective-permute-start(f32[5,1,16,128]{3,2,1,0:T(8,128)S(1)} %get-tuple-element.373), channel_id=1, source_target_pairs={{4,0},{8,4},{12,8},{16,12},{20,16},{24,20},{28,24},{0,28},{5,1},{9... | collective-permute-start | bytes 122888 | tf_op jit(solution)/shard_map/ppermute | solution.py:24
  106.5 5.6 %collective-permute-start.6 = (f32[5,6,1,128]{3,2,1,0:T(1,128)S(1)}, f32[5,6,1,128]{3,2,1,0:T(1,128)S(1)}, u32[]{:S(2)}, u32[]{:S(2)}) collective-permute-start(f32[5,6,1,128]{3,2,1,0:T(1,128)S(1)} %get-tuple-element.368), channel_id=1, source_target_pairs={{0,1},{1,2},{2,3},{3,0},{4,5},{5,6},{6,7},{7,4},{8,9},{9,10},{10,1... | collective-permute-start | bytes 46088 | tf_op jit(solution)/shard_map/ppermute | solution.py:23
  107.8 4.3 %collective-permute-start.7 = (f32[5,6,1,128]{3,2,1,0:T(1,128)S(1)}, f32[5,6,1,128]{3,2,1,0:T(1,128)S(1)}, u32[]{:S(2)}, u32[]{:S(2)}) collective-permute-start(f32[5,6,1,128]{3,2,1,0:T(1,128)S(1)} %get-tuple-element.369), channel_id=1, source_target_pairs={{1,0},{2,1},{3,2},{0,3},{5,4},{6,5},{7,6},{4,7},{9,8},{10,9},{11,1... | collective-permute-start | bytes 46088 | tf_op jit(solution)/shard_map/ppermute | solution.py:24
where the time goes:
time: 242 us; the launch traced here: 241 us
  other arithmetic  158 us (65%)
  blocking collectives  39.5 us (16%)
  loops' own time  16.1 us (7%)
  starting transfers between devices  14.4 us (6%)
  waiting for transfers between devices  6.95 us (3%)
  local copies, waits for them, and re-layouts  5.41 us (2%)
    reduce_sum x32, other arithmetic, column_rates(): force_x = force_x + jnp.sum(pressure * delta_x, axis=2)  152 us
    pmin x1, blocking collectives, body(): lowest = lax.pmin(own_lowest, ('chan', 'cross'))  39.5 us
    another operation x2, loops' own time, local_rates(): per_column = lax.map(one_column, columns)  16.1 us
    ppermute x4, starting transfers between devices, padded_2(): after = lax.ppermute(leading, axis, down)  10.2 us
    ppermute x4, waiting for transfers between devices, padded_2(): before = lax.ppermute(last, axis, up)  6.81 us
  transfers between devices with their start and end apart: 8, of which 6 were waited for; matrix products, arithmetic and copies ran while one was open for 0% of the time, Pallas kernels for 0%

commit v1 on v0

v1 whole, which is shorter than its diff:
```python
import functools
import math

import jax
import jax.numpy as jnp
from jax import lax
from jax.experimental import pallas as pl
from jax.experimental.pallas import tpu as pltpu
from jax.sharding import PartitionSpec as P

FAR_SHIFT = 8.0
SOUND_SQ = 100.0
KERNEL_GRAD = 140.0 / math.pi
PARTICLE_MASS = 1.0 / 128.0
GRAVITY = 1.0
TIME_STEP = 0.025
FORCE_SCALE = KERNEL_GRAD * PARTICLE_MASS
EMPTY_DENSITY = 1000000000.0

FEATURES = 9
QROWS = 32


def exchange(x, sides):
    for axis, dim in sides:
        size, length = (lax.axis_size(axis), x.shape[dim])
        up = [(i, (i + 1) % size) for i in range(size)]
        down = [(j, i) for i, j in up]
        last = lax.slice_in_dim(x, length - 1, length, axis=dim)
        leading = lax.slice_in_dim(x, 0, 1, axis=dim)
        before = lax.ppermute(last, axis, up)
        after = lax.ppermute(leading, axis, down)
        x = jnp.concatenate([before, x, after], axis=dim)
    return x


def extend_rims(fields):
    extended = exchange(fields, (("chan", 1), ("cross", 2)))
    cross_place = lax.axis_index("cross")
    cross_count = lax.axis_size("cross")
    rim_row = jnp.arange(extended.shape[2], dtype=jnp.int32)
    lower_open = jnp.logical_or(rim_row != 0, cross_place > 0)
    upper_open = jnp.logical_or(rim_row != extended.shape[2] - 1, cross_place < cross_count - 1)
    wall_keep = jnp.logical_and(lower_open, upper_open).astype(jnp.float32)
    return extended * wall_keep[None, None, :, None]


def split3(value):
    high = value.astype(jnp.bfloat16).astype(jnp.float32)
    rest = value - high
    middle = rest.astype(jnp.bfloat16).astype(jnp.float32)
    return high, middle, rest - middle


def rates_kernel(final, *refs):
    if final:
        padded, base, out, low, px, py, staged, feats, sums = refs
    else:
        padded, out, px, py, staged, feats, sums = refs
    _, pcols, prows, slots = padded.shape
    cols, rows = pcols - 2, prows - 2
    mid_col, mid_row = (pcols - 1) / 2.0, (prows - 1) / 2.0

    row_shift = lax.broadcasted_iota(jnp.int32, (prows, slots), 0).astype(jnp.float32) - mid_row
    staged[...] = jnp.zeros_like(staged)
    for c in range(pcols):
        x = (padded[0, c] - (FAR_SHIFT + 0.5)) + (c - mid_col)
        y = (padded[1, c] - (FAR_SHIFT + 0.5)) + row_shift
        u, v = padded[2, c], padded[3, c]
        p = SOUND_SQ * (padded[4, c] - 1.0)
        px[c] = x
        py[c] = y
        staged[:, 0, :] = jnp.ones_like(x)
        for f, value in enumerate((x, y, p, p * x, p * y, u, v, u * x + v * y)):
            for k, part in enumerate(split3(value)):
                staged[:, 1 + 3 * f + k, :] = part
        for j in range(prows):
            feats[c, :, j * slots : (j + 1) * slots] = staged[j].astype(jnp.bfloat16)

    def one_bin(n, carry):
        i = n // rows
        j = n % rows
        xa = jnp.broadcast_to(px[i + 1, pl.ds(j + 1, 1), :], (slots, slots)).T
        ya = jnp.broadcast_to(py[i + 1, pl.ds(j + 1, 1), :], (slots, slots)).T
        total = None
        for di in range(3):
            highs, lows = [], []
            for dj in range(3):
                dx = xa - px[i + di, pl.ds(j + dj, 1), :]
                dy = ya - py[i + di, pl.ds(j + dj, 1), :]
                d2 = jnp.maximum(dx * dx + dy * dy, 1e-30)
                s = jnp.maximum(1.0 - d2 * lax.rsqrt(d2), 0.0)
                w = s * s * s
                high = w.astype(jnp.bfloat16)
                highs.append(high)
                lows.append((w - high.astype(jnp.float32)).astype(jnp.bfloat16))
            q = feats[i + di, :, pl.ds(pl.multiple_of(j * slots, slots), 3 * slots)]
            part = lax.dot_general(
                jnp.concatenate(highs + lows, axis=1),
                jnp.concatenate([q, q], axis=1),
                (((1,), (1,)), ((), ())),
                preferred_element_type=jnp.float32,
            )
            total = part if total is None else total + part
        sums[n] = total.T
        return carry

    lax.fori_loop(0, cols * rows, one_bin, 0)

    lowest = None
    for i in range(cols):
        def take(f):
            block = pl.ds(i * rows, rows)
            if f == 0:
                return sums[block, 0, :]
            first = 1 + 3 * (f - 1)
            return sums[block, first, :] + (sums[block, first + 1, :] + sums[block, first + 2, :])

        s1, sx, sy, sp, spx, spy, su, sv, sc = [take(f) for f in range(FEATURES)]
        own = pl.ds(1, rows)
        x, y = px[i + 1, own, :], py[i + 1, own, :]
        u, v = padded[2, i + 1, own, :], padded[3, i + 1, own, :]
        p = SOUND_SQ * (padded[4, i + 1, own, :] - 1.0)
        away_x, away_y = x * s1 - sx, y * s1 - sy
        force_x = FORCE_SCALE * (p * away_x + (x * sp - spx))
        force_y = FORCE_SCALE * (p * away_y + (y * sp - spy)) - GRAVITY
        compress = -FORCE_SCALE * ((u * away_x + v * away_y) - (x * su + y * sv) + sc)
        occupied = padded[0, i + 1, own, :] > 0.5 * FAR_SHIFT
        half_step = 0.5 * TIME_STEP
        if final:
            bx, by, bu, bv, br = [base[k, i] for k in range(5)]
            new_u = bu + TIME_STEP * force_x
            new_v = bv + TIME_STEP * force_y
            new_rho = br + TIME_STEP * compress
            values = (
                bx + half_step * (bu + new_u) - FAR_SHIFT,
                by + half_step * (bv + new_v) - FAR_SHIFT,
                new_u,
                new_v,
                new_rho,
            )
            least = jnp.min(jnp.where(occupied, new_rho, EMPTY_DENSITY), axis=0, keepdims=True)
            lowest = least if lowest is None else jnp.minimum(lowest, least)
        else:
            values = (
                padded[0, i + 1, own, :] + half_step * u,
                padded[1, i + 1, own, :] + half_step * v,
                u + half_step * force_x,
                v + half_step * force_y,
                padded[4, i + 1, own, :] + half_step * compress,
            )
        for k, value in enumerate(values):
            out[k, i] = jnp.where(occupied, value, 0.0)
    if final:
        low[...] = jnp.broadcast_to(lowest, low.shape)


def rates_step(padded, base=None):
    count, pcols, prows, slots = padded.shape
    cols, rows = pcols - 2, prows - 2
    final = base is not None
    out_shape = [jax.ShapeDtypeStruct((count, cols, rows, slots), jnp.float32)]
    if final:
        out_shape.append(jax.ShapeDtypeStruct((8, slots), jnp.float32))
    operands = (padded, base) if final else (padded,)
    vmem = pl.BlockSpec(memory_space=pltpu.VMEM)
    pairs = 9 * cols * rows * slots * slots
    return pl.pallas_call(
        functools.partial(rates_kernel, final),
        out_shape=out_shape,
        in_specs=[vmem] * len(operands),
        out_specs=[vmem] * len(out_shape),
        scratch_shapes=[
            pltpu.VMEM((pcols, prows, slots), jnp.float32),
            pltpu.VMEM((pcols, prows, slots), jnp.float32),
            pltpu.VMEM((prows, QROWS, slots), jnp.float32),
            pltpu.VMEM((pcols, QROWS, prows * slots), jnp.bfloat16),
            pltpu.VMEM((cols * rows, QROWS, slots), jnp.float32),
        ],
        compiler_params=pltpu.CompilerParams(vmem_limit_bytes=32 * 1024 * 1024),
        cost_estimate=pl.CostEstimate(
            flops=pairs * 40, bytes_accessed=4 * 1024 * 1024, transcendentals=pairs
        ),
    )(*operands)


def body(positions, velocity, density, counts):
    slot_index = jnp.arange(positions.shape[-1], dtype=jnp.int32)
    occupied = slot_index[None, None, :] < counts[:, :, None]
    fields = jnp.concatenate([positions + FAR_SHIFT, velocity, density[None]], axis=0)
    fields = jnp.where(occupied[None], fields, 0.0)
    (predicted,) = rates_step(extend_rims(fields))
    new_fields, low = rates_step(extend_rims(predicted), fields)
    lowest = lax.pmin(jnp.min(low), ("chan", "cross"))
    return (new_fields, lowest)


def solution(mesh):
    return jax.shard_map(
        body,
        mesh=mesh,
        in_specs=(
            P(None, "chan", "cross", None),
            P(None, "chan", "cross", None),
            P("chan", "cross", None),
            P("chan", "cross"),
        ),
        out_specs=(P(None, "chan", "cross", None), P()),
        check_vma=False,
    )
```

time: 242 us -> 138 us (0.57)
  other arithmetic: 158 us -> 2.49 us
  Pallas kernels: 0 us -> 73.1 us
  loops' own time: 16.1 us -> 0 us
  local copies, waits for them, and re-layouts: 5.41 us -> 0.03 us
    reduce_sum x32 -> x0, other arithmetic: 152 us -> none  [column_rates(): force_x = force_x + jnp.sum(pressure * delta_x, axis=2)]
    pallas_call x0 -> x2, Pallas kernels: none -> 73.1 us  [rates_step(): pl.pallas_call(functools.partial(rates_kernel, final), out_shape=out_shap...]
    another operation x2 -> x0, loops' own time: 16.1 us -> none  [local_rates(): per_column = lax.map(one_column, columns)]
    dynamic_slice x8 -> x0, local copies, waits for them, and re-layouts: 4.69 us -> none  [local_rates(): per_column = lax.map(one_column, columns)]
    mul x20 -> x2, other arithmetic: 2.76 us -> 0.19 us  [extend_rims(): return extended * wall_keep[None, None, :, None]]
where the time goes in v1:
time: 138 us; the launch traced here: 137 us
  Pallas kernels  73.1 us (53%)
  blocking collectives  39.5 us (29%)
  starting transfers between devices  14.4 us (10%)
  waiting for transfers between devices  7.02 us (5%)
  other arithmetic  2.49 us (2%)
    pallas_call x2, Pallas kernels, rates_step(): pl.pallas_call(functools.partial(rates_kernel, final), out_shape=out_shap...  73.1 us
    pmin x1, blocking collectives, body(): lowest = lax.pmin(jnp.min(low), ('chan', 'cross'))  39.5 us
    ppermute x4, starting transfers between devices, exchange(): after = lax.ppermute(leading, axis, down)  10.2 us
    ppermute x4, waiting for transfers between devices, exchange(): before = lax.ppermute(last, axis, up)  6.88 us
    ppermute x4, starting transfers between devices, exchange(): before = lax.ppermute(last, axis, up)  4.2 us
  transfers between devices with their start and end apart: 8, of which 6 were waited for; matrix products, arithmetic and copies ran while one was open for 0% of the time, Pallas kernels for 0%

profile of v1, /device:TPU:0, one launch (start us, length us, event | category | flops | bytes accessed | tf_op | source)
XLA Modules:
  0.0 137.3 jit_solution(15709623959770382797)
XLA Ops:
  0.6 0.8 iota_compare_fusion
  1.4 0.0 copy-start
  1.4 0.0 copy-start.1
  1.4 0.9 broadcast_add_fusion
  2.3 0.0 copy-done
  2.3 0.0 copy-done.1
  2.3 0.5 collective-permute-start
  2.8 2.9 %collective-permute-start.1 = (f32[5,1,16,128]{3,2,1,0:T(8,128)S(1)}, f32[5,1,16,128]{3,2,1,0:T(8,128)S(1)}, u32[]{:S(2)}, u32[]{:S(2)}) collective-permute-start(f32[5,1,16,128]{3,2,1,0:T(8,128)S(1)} %get-tuple-element.13), channel_id=1, source_target_pairs={{4,0},{8,4},{12,8},{16,12},{20,16},{24,20},{28,24},{0,28},{5,1},{9... | collective-permute-start | bytes 122888 | tf_op jit(solution)/shard_map/ppermute | solution.py:32
  5.8 1.6 %collective-permute-done = f32[5,1,16,128]{3,2,1,0:T(8,128)S(1)} collective-permute-done((f32[5,1,16,128]{3,2,1,0:T(8,128)S(1)}, f32[5,1,16,128]{3,2,1,0:T(8,128)S(1)}, u32[]{:S(2)}, u32[]{:S(2)}) %collective-permute-start) | collective-permute-done | bytes 40992 | tf_op jit(solution)/shard_map/ppermute | solution.py:31
  7.4 0.1 collective-permute-done.1
  7.5 2.3 %collective-permute-start.2 = (f32[5,6,1,128]{3,2,1,0:T(1,128)S(1)}, f32[5,6,1,128]{3,2,1,0:T(1,128)S(1)}, u32[]{:S(2)}, u32[]{:S(2)}) collective-permute-start(f32[5,6,1,128]{3,2,1,0:T(1,128)S(1)} %get-tuple-element.8), channel_id=1, source_target_pairs={{0,1},{1,2},{2,3},{3,0},{4,5},{5,6},{6,7},{7,4},{8,9},{9,10},{10,1... | collective-permute-start | bytes 46088 | tf_op jit(solution)/shard_map/ppermute | solution.py:31
  9.8 2.1 %collective-permute-start.3 = (f32[5,6,1,128]{3,2,1,0:T(1,128)S(1)}, f32[5,6,1,128]{3,2,1,0:T(1,128)S(1)}, u32[]{:S(2)}, u32[]{:S(2)}) collective-permute-start(f32[5,6,1,128]{3,2,1,0:T(1,128)S(1)} %get-tuple-element.9), channel_id=1, source_target_pairs={{1,0},{2,1},{3,2},{0,3},{5,4},{6,5},{7,6},{4,7},{9,8},{10,9},{11,1... | collective-permute-start | bytes 46088 | tf_op jit(solution)/shard_map/ppermute | solution.py:32
  11.9 1.9 %collective-permute-done.2 = f32[5,6,1,128]{3,2,1,0:T(1,128)S(1)} collective-permute-done((f32[5,6,1,128]{3,2,1,0:T(1,128)S(1)}, f32[5,6,1,128]{3,2,1,0:T(1,128)S(1)}, u32[]{:S(2)}, u32[]{:S(2)}) %collective-permute-start.2) | collective-permute-done | bytes 15392 | tf_op jit(solution)/shard_map/ppermute | solution.py:31
  13.8 0.1 collective-permute-done.3
  13.9 0.1 maximum_multiply_fusion.refs_0_
  14.0 36.2 %shard_map.59 = f32[5,4,16,128]{3,2,1,0:T(8,128)S(1)} custom-call(f32[5,6,18,128]{3,2,1,0:T(8,128)S(1)} %maximum_multiply_fusion.refs_0_), custom_call_target="tpu_custom_call" | custom-call | flops 377487360 | bytes 4194304 | tf_op jit(solution)/shard_map/pallas_call | solution.py:168
  50.2 0.1 collective-permute-start.4
  50.3 2.6 %collective-permute-start.5 = (f32[5,1,16,128]{3,2,1,0:T(8,128)S(1)}, f32[5,1,16,128]{3,2,1,0:T(8,128)S(1)}, u32[]{:S(2)}, u32[]{:S(2)}) collective-permute-start(f32[5,1,16,128]{3,2,1,0:T(8,128)S(1)} %get-tuple-element.11), channel_id=1, source_target_pairs={{4,0},{8,4},{12,8},{16,12},{20,16},{24,20},{28,24},{0,28},{5,1},{9... | collective-permute-start | bytes 122888 | tf_op jit(solution)/shard_map/ppermute | solution.py:32
  52.9 1.7 %collective-permute-done.4 = f32[5,1,16,128]{3,2,1,0:T(8,128)S(1)} collective-permute-done((f32[5,1,16,128]{3,2,1,0:T(8,128)S(1)}, f32[5,1,16,128]{3,2,1,0:T(8,128)S(1)}, u32[]{:S(2)}, u32[]{:S(2)}) %collective-permute-start.4) | collective-permute-done | bytes 40992 | tf_op jit(solution)/shard_map/ppermute | solution.py:31
  54.6 0.0 collective-permute-done.5
  54.6 1.3 collective-permute-start.6
  55.9 2.6 %collective-permute-start.7 = (f32[5,6,1,128]{3,2,1,0:T(1,128)S(1)}, f32[5,6,1,128]{3,2,1,0:T(1,128)S(1)}, u32[]{:S(2)}, u32[]{:S(2)}) collective-permute-start(f32[5,6,1,128]{3,2,1,0:T(1,128)S(1)} %get-tuple-element.7), channel_id=1, source_target_pairs={{1,0},{2,1},{3,2},{0,3},{5,4},{6,5},{7,6},{4,7},{9,8},{10,9},{11,1... | collective-permute-start | bytes 46088 | tf_op jit(solution)/shard_map/ppermute | solution.py:32
  58.5 1.7 %collective-permute-done.6 = f32[5,6,1,128]{3,2,1,0:T(1,128)S(1)} collective-permute-done((f32[5,6,1,128]{3,2,1,0:T(1,128)S(1)}, f32[5,6,1,128]{3,2,1,0:T(1,128)S(1)}, u32[]{:S(2)}, u32[]{:S(2)}) %collective-permute-start.6) | collective-permute-done | bytes 15392 | tf_op jit(solution)/shard_map/ppermute | solution.py:31
  60.2 0.0 collective-permute-done.7
  60.2 0.1 maximum_multiply_fusion.1.refs_0_
  60.3 36.9 %shard_map.60 = (f32[5,4,16,128]{3,2,1,0:T(8,128)}, f32[8,128]{1,0:T(8,128)S(1)}) custom-call(f32[5,6,18,128]{3,2,1,0:T(8,128)S(1)} %maximum_multiply_fusion.1.refs_0_, f32[5,4,16,128]{3,2,1,0:T(8,128)S(1)} %maximum_select_fusion.refs_1_), custom_call_target="tpu_custom_call" | custom-call | flops 377487360 | bytes 4194304 | tf_op jit(solution)/shard_map/pallas_call | solution.py:168
  97.2 0.6 reduce_min.9
  97.8 39.5 %pmin.7 = f32[]{:T(128)} all-reduce(f32[]{:T(128)} %reduce_min.9), channel_id=1, replica_groups=mesh['chan'=8,'cross'=4] {'chan','cross'}, use_global_device_ids=true, to_apply=%region_1.2 | all-reduce | flops 1 | bytes 8 | tf_op jit(solution)/shard_map/pmin | solution.py:194
  (6 shorter events, 0.1 us)
Async XLA Ops:
  1.4 0.9 copy-start
  1.4 0.9 copy-start.1
  2.3 5.1 %collective-permute-start = (f32[5,1,16,128]{3,2,1,0:T(8,128)S(1)}, f32[5,1,16,128]{3,2,1,0:T(8,128)S(1)}, u32[]{:S(2)}, u32[]{:S(2)}) collective-permute-start(f32[5,1,16,128]{3,2,1,0:T(8,128)S(1)} %get-tuple-element.12), channel_id=1, source_target_pairs={{0,4},{4,8},{8,12},{12,16},{16,20},{20,24},{24,28},{28,0},{1,5},{5... | collective-permute-start | bytes 122888 | tf_op jit(solution)/shard_map/ppermute | solution.py:31
  2.8 4.6 %collective-permute-start.1 = (f32[5,1,16,128]{3,2,1,0:T(8,128)S(1)}, f32[5,1,16,128]{3,2,1,0:T(8,128)S(1)}, u32[]{:S(2)}, u32[]{:S(2)}) collective-permute-start(f32[5,1,16,128]{3,2,1,0:T(8,128)S(1)} %get-tuple-element.13), channel_id=1, source_target_pairs={{4,0},{8,4},{12,8},{16,12},{20,16},{24,20},{28,24},{0,28},{5,1},{9... | collective-permute-start | bytes 122888 | tf_op jit(solution)/shard_map/ppermute | solution.py:32
  7.5 6.3 %collective-permute-start.2 = (f32[5,6,1,128]{3,2,1,0:T(1,128)S(1)}, f32[5,6,1,128]{3,2,1,0:T(1,128)S(1)}, u32[]{:S(2)}, u32[]{:S(2)}) collective-permute-start(f32[5,6,1,128]{3,2,1,0:T(1,128)S(1)} %get-tuple-element.8), channel_id=1, source_target_pairs={{0,1},{1,2},{2,3},{3,0},{4,5},{5,6},{6,7},{7,4},{8,9},{9,10},{10,1... | collective-permute-start | bytes 46088 | tf_op jit(solution)/shard_map/ppermute | solution.py:31
  9.8 4.1 %collective-permute-start.3 = (f32[5,6,1,128]{3,2,1,0:T(1,128)S(1)}, f32[5,6,1,128]{3,2,1,0:T(1,128)S(1)}, u32[]{:S(2)}, u32[]{:S(2)}) collective-permute-start(f32[5,6,1,128]{3,2,1,0:T(1,128)S(1)} %get-tuple-element.9), channel_id=1, source_target_pairs={{1,0},{2,1},{3,2},{0,3},{5,4},{6,5},{7,6},{4,7},{9,8},{10,9},{11,1... | collective-permute-start | bytes 46088 | tf_op jit(solution)/shard_map/ppermute | solution.py:32
  50.2 4.4 %collective-permute-start.4 = (f32[5,1,16,128]{3,2,1,0:T(8,128)S(1)}, f32[5,1,16,128]{3,2,1,0:T(8,128)S(1)}, u32[]{:S(2)}, u32[]{:S(2)}) collective-permute-start(f32[5,1,16,128]{3,2,1,0:T(8,128)S(1)} %get-tuple-element.10), channel_id=1, source_target_pairs={{0,4},{4,8},{8,12},{12,16},{16,20},{20,24},{24,28},{28,0},{1,5},{5... | collective-permute-start | bytes 122888 | tf_op jit(solution)/shard_map/ppermute | solution.py:31
  50.3 4.3 %collective-permute-start.5 = (f32[5,1,16,128]{3,2,1,0:T(8,128)S(1)}, f32[5,1,16,128]{3,2,1,0:T(8,128)S(1)}, u32[]{:S(2)}, u32[]{:S(2)}) collective-permute-start(f32[5,1,16,128]{3,2,1,0:T(8,128)S(1)} %get-tuple-element.11), channel_id=1, source_target_pairs={{4,0},{8,4},{12,8},{16,12},{20,16},{24,20},{28,24},{0,28},{5,1},{9... | collective-permute-start | bytes 122888 | tf_op jit(solution)/shard_map/ppermute | solution.py:32
  54.6 5.6 %collective-permute-start.6 = (f32[5,6,1,128]{3,2,1,0:T(1,128)S(1)}, f32[5,6,1,128]{3,2,1,0:T(1,128)S(1)}, u32[]{:S(2)}, u32[]{:S(2)}) collective-permute-start(f32[5,6,1,128]{3,2,1,0:T(1,128)S(1)} %get-tuple-element.6), channel_id=1, source_target_pairs={{0,1},{1,2},{2,3},{3,0},{4,5},{5,6},{6,7},{7,4},{8,9},{9,10},{10,1... | collective-permute-start | bytes 46088 | tf_op jit(solution)/shard_map/ppermute | solution.py:31
  55.9 4.3 %collective-permute-start.7 = (f32[5,6,1,128]{3,2,1,0:T(1,128)S(1)}, f32[5,6,1,128]{3,2,1,0:T(1,128)S(1)}, u32[]{:S(2)}, u32[]{:S(2)}) collective-permute-start(f32[5,6,1,128]{3,2,1,0:T(1,128)S(1)} %get-tuple-element.7), channel_id=1, source_target_pairs={{1,0},{2,1},{3,2},{0,3},{5,4},{6,5},{7,6},{4,7},{9,8},{10,9},{11,1... | collective-permute-start | bytes 46088 | tf_op jit(solution)/shard_map/ppermute | solution.py:32

commit v2 on v1

--- a/solution.py
+++ b/solution.py
@@ -19,30 +19,169 @@
 
 FEATURES = 9
 QROWS = 32
-
-
-def exchange(x, sides):
-    for axis, dim in sides:
-        size, length = (lax.axis_size(axis), x.shape[dim])
-        up = [(i, (i + 1) % size) for i in range(size)]
-        down = [(j, i) for i, j in up]
-        last = lax.slice_in_dim(x, length - 1, length, axis=dim)
-        leading = lax.slice_in_dim(x, 0, 1, axis=dim)
-        before = lax.ppermute(last, axis, up)
-        after = lax.ppermute(leading, axis, down)
-        x = jnp.concatenate([before, x, after], axis=dim)
-    return x
-
-
-def extend_rims(fields):
-    extended = exchange(fields, (("chan", 1), ("cross", 2)))
-    cross_place = lax.axis_index("cross")
-    cross_count = lax.axis_size("cross")
-    rim_row = jnp.arange(extended.shape[2], dtype=jnp.int32)
-    lower_open = jnp.logical_or(rim_row != 0, cross_place > 0)
-    upper_open = jnp.logical_or(rim_row != extended.shape[2] - 1, cross_place < cross_count - 1)
-    wall_keep = jnp.logical_and(lower_open, upper_open).astype(jnp.float32)
-    return extended * wall_keep[None, None, :, None]
+MESH = pl.DeviceIdType.MESH
+BINS_AT_ONCE = 2
+CHUNK = 32
+
+
+def halo_kernel(fields, padded, top, bottom, land_chan, land_cross, send_sems, recv_sems):
+    _, cols, rows, _ = fields.shape
+    chan, cross = lax.axis_index("chan"), lax.axis_index("cross")
+    chans, crosses = lax.axis_size("chan"), lax.axis_size("cross")
+    around = [lax.rem(chan + (chans - 1), chans), chan, lax.rem(chan + 1, chans)]
+    above, below = lax.rem(cross + 1, crosses), lax.rem(cross + (crosses - 1), crosses)
+    has_above, has_below = cross < crosses - 1, cross > 0
+
+    barrier = pltpu.get_barrier_semaphore()
+    for place in (around[0], around[2]):
+        pl.semaphore_signal(barrier, inc=1, device_id=(place, cross), device_id_type=MESH)
+    for there, row in ((has_above, above), (has_below, below)):
+        @pl.when(there)
+        def _():
+            for place in around:
+                pl.semaphore_signal(barrier, inc=1, device_id=(place, row), device_id_type=MESH)
+
+    top[...] = jnp.zeros_like(top)
+    bottom[...] = jnp.zeros_like(bottom)
+    top[:, 0:cols, :] = fields[:, :, rows - 1, :]
+    bottom[:, 0:cols, :] = fields[:, :, 0, :]
+    pl.semaphore_wait(
+        barrier, 2 + 3 * has_above.astype(jnp.int32) + 3 * has_below.astype(jnp.int32)
+    )
+
+    def remote(src, dst, slot, place, row):
+        return pltpu.make_async_remote_copy(
+            src_ref=src,
+            dst_ref=dst,
+            send_sem=send_sems.at[slot],
+            recv_sem=recv_sems.at[slot],
+            device_id=(place, row),
+            device_id_type=MESH,
+        )
+
+    upward = [remote(top, land_cross.at[k], k, around[2 - k], above) for k in range(3)]
+    downward = [remote(bottom, land_cross.at[3 + k], 3 + k, around[2 - k], below) for k in range(3)]
+    sideways = [
+        remote(fields.at[:, cols - 1], land_chan.at[0], 6, around[2], cross),
+        remote(fields.at[:, 0], land_chan.at[1], 7, around[0], cross),
+    ]
+
+    @pl.when(has_above)
+    def _():
+        for copy in upward:
+            copy.start()
+
+    @pl.when(has_below)
+    def _():
+        for copy in downward:
+            copy.start()
+
+    for copy in sideways:
+        copy.start()
+
+    padded[:, 1 : cols + 1, 1 : rows + 1, :] = fields[...]
+    for copy in sideways:
+        copy.wait()
+    padded[:, 0, 1 : rows + 1, :] = land_chan[0]
+    padded[:, cols + 1, 1 : rows + 1, :] = land_chan[1]
+
+    for here, there, arriving, leaving, first, rim in (
+        (has_below, has_above, upward, upward, 0, 0),
+        (has_above, has_below, downward, downward, 3, rows + 1),
+    ):
+        @pl.when(here)
+        def _():
+            for copy in arriving:
+                copy.wait_recv()
+            padded[:, 0, rim, :] = land_cross[first, :, cols - 1, :]
+            padded[:, 1 : cols + 1, rim, :] = land_cross[first + 1, :, 0:cols, :]
+            padded[:, cols + 1, rim, :] = land_cross[first + 2, :, 0, :]
+
+        @pl.when(jnp.logical_not(here))
+        def _():
+            padded[:, :, rim, :] = jnp.zeros_like(padded[:, :, rim, :])
+
+        @pl.when(there)
+        def _():
+            for copy in leaving:
+                copy.wait_send()
+
+
+def extend_rims(fields, collective_id):
+    count, cols, rows, slots = fields.shape
+    sublanes = -(-cols // 8) * 8
+    vmem = pl.BlockSpec(memory_space=pltpu.VMEM)
+    return pl.pallas_call(
+        halo_kernel,
+        out_shape=jax.ShapeDtypeStruct((count, cols + 2, rows + 2, slots), jnp.float32),
+        in_specs=[vmem],
+        out_specs=vmem,
+        scratch_shapes=[
+            pltpu.VMEM((count, sublanes, slots), jnp.float32),
+            pltpu.VMEM((count, sublanes, slots), jnp.float32),
+            pltpu.VMEM((2, count, rows, slots), jnp.float32),
+            pltpu.VMEM((6, count, sublanes, slots), jnp.float32),
+            pltpu.SemaphoreType.DMA((8,)),
+            pltpu.SemaphoreType.DMA((8,)),
+        ],
+        compiler_params=pltpu.CompilerParams(collective_id=collective_id, has_side_effects=True),
+    )(fields)
+
+
+def lowest_kernel(low, out, mine, land_chan, land_cross, send_sems, recv_sems):
+    chan, cross = lax.axis_index("chan"), lax.axis_index("cross")
+    chans, crosses = lax.axis_size("chan"), lax.axis_size("cross")
+    along = [(lax.rem(chan + k, chans), cross) for k in range(1, chans)]
+    across = [(chan, lax.rem(cross + k, crosses)) for k in range(1, crosses)]
+    barrier = pltpu.get_barrier_semaphore()
+    for place in along + across:
+        pl.semaphore_signal(barrier, inc=1, device_id=place, device_id_type=MESH)
+    pl.semaphore_wait(barrier, len(along) + len(across))
+
+    def gather(src, land, first, places):
+        copies = [
+            pltpu.make_async_remote_copy(
+                src_ref=src,
+                dst_ref=land.at[k],
+                send_sem=send_sems.at[first + k],
+                recv_sem=recv_sems.at[first + k],
+                device_id=place,
+                device_id_type=MESH,
+            )
+            for k, place in enumerate(places)
+        ]
+        for copy in copies:
+            copy.start()
+        for copy in copies:
+            copy.wait()
+        least = src[...]
+        for k in range(len(places)):
+            least = jnp.minimum(least, land[k])
+        return least
+
+    mine[...] = gather(low, land_chan, 0, along)
+    least = gather(mine, land_cross, len(along), across)
+    out[...] = jnp.broadcast_to(jnp.min(least, keepdims=True), out.shape)
+
+
+def lowest_everywhere(low, collective_id):
+    chans, crosses = lax.axis_size("chan"), lax.axis_size("cross")
+    vmem = pl.BlockSpec(memory_space=pltpu.VMEM)
+    peers = chans + crosses - 2
+    return pl.pallas_call(
+        lowest_kernel,
+        out_shape=jax.ShapeDtypeStruct(low.shape, jnp.float32),
+        in_specs=[vmem],
+        out_specs=vmem,
+        scratch_shapes=[
+            pltpu.VMEM(low.shape, jnp.float32),
+            pltpu.VMEM((chans - 1,) + low.shape, jnp.float32),
+            pltpu.VMEM((crosses - 1,) + low.shape, jnp.float32),
+            pltpu.SemaphoreType.DMA((peers,)),
+            pltpu.SemaphoreType.DMA((peers,)),
+        ],
+        compiler_params=pltpu.CompilerParams(collective_id=collective_id, has_side_effects=True),
+    )(low)
 
 
 def split3(value):
@@ -77,35 +216,47 @@
         for j in range(prows):
             feats[c, :, j * slots : (j + 1) * slots] = staged[j].astype(jnp.bfloat16)
 
-    def one_bin(n, carry):
-        i = n // rows
-        j = n % rows
-        xa = jnp.broadcast_to(px[i + 1, pl.ds(j + 1, 1), :], (slots, slots)).T
-        ya = jnp.broadcast_to(py[i + 1, pl.ds(j + 1, 1), :], (slots, slots)).T
-        total = None
+    at_once = math.gcd(BINS_AT_ONCE, cols * rows)
+
+    def some_bins(step, carry):
+        places = []
+        for k in range(at_once):
+            n = step * at_once + k
+            i, j = n // rows, n % rows
+            xa = jnp.broadcast_to(px[i + 1, pl.ds(j + 1, 1), :], (slots, slots)).T
+            ya = jnp.broadcast_to(py[i + 1, pl.ds(j + 1, 1), :], (slots, slots)).T
+            places.append((n, i, j, xa, ya))
+        totals = [None] * at_once
         for di in range(3):
-            highs, lows = [], []
-            for dj in range(3):
-                dx = xa - px[i + di, pl.ds(j + dj, 1), :]
-                dy = ya - py[i + di, pl.ds(j + dj, 1), :]
-                d2 = jnp.maximum(dx * dx + dy * dy, 1e-30)
-                s = jnp.maximum(1.0 - d2 * lax.rsqrt(d2), 0.0)
-                w = s * s * s
-                high = w.astype(jnp.bfloat16)
-                highs.append(high)
-                lows.append((w - high.astype(jnp.float32)).astype(jnp.bfloat16))
-            q = feats[i + di, :, pl.ds(pl.multiple_of(j * slots, slots), 3 * slots)]
-            part = lax.dot_general(
-                jnp.concatenate(highs + lows, axis=1),
-                jnp.concatenate([q, q], axis=1),
-                (((1,), (1,)), ((), ())),
-                preferred_element_type=jnp.float32,
-            )
-            total = part if total is None else total + part
-        sums[n] = total.T
+            for k, (n, i, j, xa, ya) in enumerate(places):
+                xb = [px[i + di, pl.ds(j + dj, 1), :] for dj in range(3)]
+                yb = [py[i + di, pl.ds(j + dj, 1), :] for dj in range(3)]
+                weights = []
+                for a in range(0, slots, CHUNK):
+                    highs, lows = [], []
+                    for dj in range(3):
+                        dx = xa[a : a + CHUNK] - xb[dj]
+                        dy = ya[a : a + CHUNK] - yb[dj]
+                        d2 = jnp.maximum(dx * dx + dy * dy, 1e-30)
+                        s = jnp.maximum(1.0 - d2 * lax.rsqrt(d2), 0.0)
+                        w = s * s * s
+                        high = w.astype(jnp.bfloat16)
+                        highs.append(high)
+                        lows.append((w - high.astype(jnp.float32)).astype(jnp.bfloat16))
+                    weights.append(jnp.concatenate(highs + lows, axis=1))
+                q = feats[i + di, :, pl.ds(pl.multiple_of(j * slots, slots), 3 * slots)]
+                part = lax.dot_general(
+                    jnp.concatenate(weights, axis=0),
+                    jnp.concatenate([q, q], axis=1),
+                    (((1,), (1,)), ((), ())),
+                    preferred_element_type=jnp.float32,
+                )
+                totals[k] = part if di == 0 else totals[k] + part
+        for k, (n, i, j, xa, ya) in enumerate(places):
+            sums[n] = totals[k].T
         return carry
 
-    lax.fori_loop(0, cols * rows, one_bin, 0)
+    lax.fori_loop(0, cols * rows // at_once, some_bins, 0)
 
     lowest = None
     for i in range(cols):
@@ -189,10 +340,9 @@
     occupied = slot_index[None, None, :] < counts[:, :, None]
     fields = jnp.concatenate([positions + FAR_SHIFT, velocity, density[None]], axis=0)
     fields = jnp.where(occupied[None], fields, 0.0)
-    (predicted,) = rates_step(extend_rims(fields))
-    new_fields, low = rates_step(extend_rims(predicted), fields)
-    lowest = lax.pmin(jnp.min(low), ("chan", "cross"))
-    return (new_fields, lowest)
+    (predicted,) = rates_step(extend_rims(fields, 0))
+    new_fields, low = rates_step(extend_rims(predicted, 1), fields)
+    return (new_fields, lowest_everywhere(low, 2)[0, 0])
 
 
 def solution(mesh):

time: 138 us -> 94.8 us (0.69)
  blocking collectives: 39.5 us -> 0 us
  starting transfers between devices: 14.4 us -> 0 us
  Pallas kernels: 73.1 us -> 87 us
  waiting for transfers between devices: 7.02 us -> 0 us
  local copies, waits for them, and re-layouts: 0.03 us -> 4.42 us
    pmin x1 -> x0, blocking collectives: 39.5 us -> none  [body(): lowest = lax.pmin(jnp.min(low), ('chan', 'cross'))]
    pallas_call x0 -> x3, Pallas kernels: none -> 27.9 us  [the longest x2 17.4 us: extend_rims(): pl.pallas_call(halo_kernel, out_shape=jax.ShapeDtypeStruct((count, cols +...]
    ppermute x8 -> x0, starting transfers between devices: 14.4 us -> none  [the longest x4 10.2 us: exchange(): after = lax.ppermute(leading, axis, down)]
    pallas_call x2, Pallas kernels: 73.1 us -> 59.1 us  [rates_step(): pl.pallas_call(functools.partial(rates_kernel, final), out_shape=out_shap...]
    ppermute x8 -> x0, waiting for transfers between devices: 7.02 us -> none  [the longest x4 6.88 us: exchange(): before = lax.ppermute(last, axis, up)]
    unnamed x4 -> x14, local copies, waits for them, and re-layouts: 0.01 us -> 3.23 us
  transfers between devices with their start and end apart: 8 -> 0, of which waited for: 6 -> 0; matrix products, arithmetic and copies ran while one was open for 0% -> 0% of each run, Pallas kernels for 0% -> 0%
where the time goes in v2:
time: 94.8 us; the launch traced here: 94.4 us
  Pallas kernels  87 us (92%)
  local copies, waits for them, and re-layouts  4.42 us (5%)
  other arithmetic  2.32 us (2%)
    pallas_call x2, Pallas kernels, rates_step(): pl.pallas_call(functools.partial(rates_kernel, final), out_shape=out_shap...  59.1 us
    pallas_call x2, Pallas kernels, extend_rims(): pl.pallas_call(halo_kernel, out_shape=jax.ShapeDtypeStruct((count, cols +...  17.4 us
    pallas_call x1, Pallas kernels, lowest_everywhere(): pl.pallas_call(lowest_kernel, out_shape=jax.ShapeDtypeStruct(low.shape, j...  10.5 us
    unnamed x14, local copies, waits for them, and re-layouts  3.23 us

profile of v2, /device:TPU:0, one launch (start us, length us, event | category | flops | bytes accessed | tf_op | source)
XLA Modules:
  0.0 94.4 jit_solution(4279531942200524745)
XLA Ops:
  0.6 0.8 iota_compare_fusion
  1.4 0.0 copy-start.5
  1.4 0.0 copy-start.6
  1.4 0.9 broadcast_add_fusion
  2.3 0.0 copy-done.5
  2.3 0.0 copy-done.6
  2.3 0.7 maximum_select_fusion.fields.refs_1_
  3.0 9.7 %shard_map.59.refs_0_ = f32[5,6,18,128]{3,2,1,0:T(8,128)} custom-call(f32[5,4,16,128]{3,2,1,0:T(8,128)} %maximum_select_fusion.fields.refs_1_), custom_call_target="tpu_custom_call" | custom-call | tf_op jit(solution)/shard_map/pallas_call | solution.py:114
  12.7 0.0 copy-start.2
  12.7 1.0 %copy-done.2 = f32[5,6,18,128]{3,2,1,0:T(8,128)S(1)} copy-done((f32[5,6,18,128]{3,2,1,0:T(8,128)S(1)}, f32[5,6,18,128]{3,2,1,0:T(8,128)}, u32[]{:S(2)}) %copy-start.2) | copy-done | bytes 276504
  13.7 29.2 %shard_map.60.fields = f32[5,4,16,128]{3,2,1,0:T(8,128)S(1)} custom-call(f32[5,6,18,128]{3,2,1,0:T(8,128)S(1)} %copy-done.2), custom_call_target="tpu_custom_call" | custom-call | flops 377487360 | bytes 4194304 | tf_op jit(solution)/shard_map/pallas_call | solution.py:319
  42.9 0.0 copy-start.3
  42.9 0.7 copy-done.3
  43.6 0.0 copy-start
  43.6 7.7 %shard_map.61.refs_0_ = f32[5,6,18,128]{3,2,1,0:T(8,128)} custom-call(f32[5,4,16,128]{3,2,1,0:T(8,128)} %copy-done.3), custom_call_target="tpu_custom_call" | custom-call | tf_op jit(solution)/shard_map/pallas_call | solution.py:114
  51.3 0.0 copy-done
  51.3 0.0 copy-start.1
  51.3 1.0 %copy-done.1 = f32[5,6,18,128]{3,2,1,0:T(8,128)S(1)} copy-done((f32[5,6,18,128]{3,2,1,0:T(8,128)S(1)}, f32[5,6,18,128]{3,2,1,0:T(8,128)}, u32[]{:S(2)}) %copy-start.1) | copy-done | bytes 276504
  52.3 29.9 %shard_map.62 = (f32[5,4,16,128]{3,2,1,0:T(8,128)}, f32[8,128]{1,0:T(8,128)S(1)}) custom-call(f32[5,6,18,128]{3,2,1,0:T(8,128)S(1)} %copy-done.1, f32[5,4,16,128]{3,2,1,0:T(8,128)S(1)} %copy-done), custom_call_target="tpu_custom_call" | custom-call | flops 377487360 | bytes 4194304 | tf_op jit(solution)/shard_map/pallas_call | solution.py:319
  82.2 0.0 copy-start.4
  82.2 0.6 copy-done.4
  82.8 10.5 %shard_map.63 = f32[8,128]{1,0:T(8,128)} custom-call(f32[8,128]{1,0:T(8,128)} %copy-done.4), custom_call_target="tpu_custom_call" | custom-call | tf_op jit(solution)/shard_map/pallas_call | solution.py:171
  93.2 1.2 %slice.3 = f32[1,1]{1,0:T(1,128)} slice(f32[8,128]{1,0:T(8,128)} %shard_map.63), slice={[0:1], [0:1]} | slice | bytes 8 | tf_op jit(solution)/shard_map/slice | solution.py:345
Async XLA Ops:
  1.4 0.9 copy-start.5
  1.4 0.9 copy-start.6
  12.7 1.0 %copy-start.2 = (f32[5,6,18,128]{3,2,1,0:T(8,128)S(1)}, f32[5,6,18,128]{3,2,1,0:T(8,128)}, u32[]{:S(2)}) copy-start(f32[5,6,18,128]{3,2,1,0:T(8,128)} %shard_map.59.refs_0_) | copy-start | bytes 829444
  42.9 0.7 copy-start.3
  43.6 7.7 %copy-start = (f32[5,4,16,128]{3,2,1,0:T(8,128)S(1)}, f32[5,4,16,128]{3,2,1,0:T(8,128)}, u32[]{:S(2)}) copy-start(f32[5,4,16,128]{3,2,1,0:T(8,128)} %maximum_select_fusion.fields.refs_1_) | copy-start | bytes 491524
  51.3 1.0 %copy-start.1 = (f32[5,6,18,128]{3,2,1,0:T(8,128)S(1)}, f32[5,6,18,128]{3,2,1,0:T(8,128)}, u32[]{:S(2)}) copy-start(f32[5,6,18,128]{3,2,1,0:T(8,128)} %shard_map.61.refs_0_) | copy-start | bytes 829444
  82.2 0.6 copy-start.4

commit v3 on v1

v3 whole, which is shorter than its diff:
```python
import math

import jax
import jax.numpy as jnp
from jax import lax
from jax.experimental import pallas as pl
from jax.experimental.pallas import tpu as pltpu
from jax.sharding import PartitionSpec as P

FAR_SHIFT = 8.0
SOUND_SQ = 100.0
KERNEL_GRAD = 140.0 / math.pi
PARTICLE_MASS = 1.0 / 128.0
GRAVITY = 1.0
TIME_STEP = 0.025
FORCE_SCALE = KERNEL_GRAD * PARTICLE_MASS
EMPTY_DENSITY = 1000000000.0

FEATURES = 9
QROWS = 32
MESH = pl.DeviceIdType.MESH
BINS_AT_ONCE = 2
CHUNK = 32


def split3(value):
    high = value.astype(jnp.bfloat16).astype(jnp.float32)
    rest = value - high
    middle = rest.astype(jnp.bfloat16).astype(jnp.float32)
    return high, middle, rest - middle


def step_kernel(
    fields, out, low, padded, predicted, tops, bottoms, lands_chan, lands_cross,
    px, py, staged, feats, sums, mine, low_chan, low_cross,
    send_sems, recv_sems, low_send, low_recv,
):
    _, cols, rows, slots = fields.shape
    pcols, prows = cols + 2, rows + 2
    mid_col, mid_row = (pcols - 1) / 2.0, (prows - 1) / 2.0
    chan, cross = lax.axis_index("chan"), lax.axis_index("cross")
    chans, crosses = lax.axis_size("chan"), lax.axis_size("cross")
    around = [lax.rem(chan + (chans - 1), chans), chan, lax.rem(chan + 1, chans)]
    above, below = lax.rem(cross + 1, crosses), lax.rem(cross + (crosses - 1), crosses)
    has_above, has_below = cross < crosses - 1, cross > 0
    along = [(lax.rem(chan + k, chans), cross) for k in range(1, chans)]
    across = [(chan, lax.rem(cross + k, crosses)) for k in range(1, crosses)]

    barrier = pltpu.get_barrier_semaphore()
    for place in along + across:
        pl.semaphore_signal(barrier, inc=1, device_id=place, device_id_type=MESH)
    for there, row in ((has_above, above), (has_below, below)):
        @pl.when(there)
        def _():
            for place in (around[0], around[2]):
                pl.semaphore_signal(barrier, inc=1, device_id=(place, row), device_id_type=MESH)

    def remote(src, dst, send, recv, place):
        return pltpu.make_async_remote_copy(
            src_ref=src, dst_ref=dst, send_sem=send, recv_sem=recv,
            device_id=place, device_id_type=MESH,
        )

    def halo(source, stage):
        top, bottom = tops.at[stage], bottoms.at[stage]
        land_chan, land_cross = lands_chan.at[stage], lands_cross.at[stage]

        def one(src, dst, slot, place):
            return remote(src, dst, send_sems.at[stage, slot], recv_sems.at[stage, slot], place)

        upward = [one(top, land_cross.at[k], k, (around[2 - k], above)) for k in range(3)]
        downward = [
            one(bottom, land_cross.at[3 + k], 3 + k, (around[2 - k], below)) for k in range(3)
        ]
        sideways = [
            one(source.at[:, cols - 1], land_chan.at[0], 6, (around[2], cross)),
            one(source.at[:, 0], land_chan.at[1], 7, (around[0], cross)),
        ]
        return upward, downward, sideways

    def fill_rims(source, stage):
        top, bottom = tops.at[stage], bottoms.at[stage]
        top[...] = jnp.zeros_like(top)
        bottom[...] = jnp.zeros_like(bottom)
        top[:, 0:cols, :] = source[:, :, rows - 1, :]
        bottom[:, 0:cols, :] = source[:, :, 0, :]

    def send(copies):
        upward, downward, sideways = copies

        @pl.when(has_above)
        def _():
            for copy in upward:
                copy.start()

        @pl.when(has_below)
        def _():
            for copy in downward:
                copy.start()

        for copy in sideways:
            copy.start()

    def receive(copies, stage):
        upward, downward, sideways = copies
        land_chan, land_cross = lands_chan.at[stage], lands_cross.at[stage]
        for copy in sideways:
            copy.wait()
        padded[:, 0, 1 : rows + 1, :] = land_chan[0]
        padded[:, cols + 1, 1 : rows + 1, :] = land_chan[1]
        for here, there, moving, first, rim in (
            (has_below, has_above, upward, 0, 0),
            (has_above, has_below, downward, 3, rows + 1),
        ):
            @pl.when(here)
            def _():
                for copy in moving:
                    copy.wait_recv()
                padded[:, 0, rim, :] = land_cross[first, :, cols - 1, :]
                padded[:, 1 : cols + 1, rim, :] = land_cross[first + 1, :, 0:cols, :]
                padded[:, cols + 1, rim, :] = land_cross[first + 2, :, 0, :]

            @pl.when(there)
            def _():
                for copy in moving:
                    copy.wait_send()

    row_shift = lax.broadcasted_iota(jnp.int32, (prows, slots), 0).astype(jnp.float32) - mid_row

    def build(first, last):
        for c in range(first, last):
            x = (padded[0, c] - (FAR_SHIFT + 0.5)) + (c - mid_col)
            y = (padded[1, c] - (FAR_SHIFT + 0.5)) + row_shift
            u, v = padded[2, c], padded[3, c]
            p = SOUND_SQ * (padded[4, c] - 1.0)
            px[c] = x
            py[c] = y
            staged[:, 0, :] = jnp.ones_like(x)
            for f, value in enumerate((x, y, p, p * x, p * y, u, v, u * x + v * y)):
                for k, part in enumerate(split3(value)):
                    staged[:, 1 + 3 * f + k, :] = part
            for j in range(prows):
                feats[c, :, j * slots : (j + 1) * slots] = staged[j].astype(jnp.bfloat16)

    def sum_bins(count, bin_of):
        at_once = math.gcd(BINS_AT_ONCE, count)

        def some_bins(step, carry):
            places = []
            for k in range(at_once):
                i, j = bin_of(step * at_once + k)
                xa = jnp.broadcast_to(px[i + 1, pl.ds(j + 1, 1), :], (slots, slots)).T
                ya = jnp.broadcast_to(py[i + 1, pl.ds(j + 1, 1), :], (slots, slots)).T
                places.append((i, j, jnp.concatenate([xa] * 3, 1), jnp.concatenate([ya] * 3, 1)))
            totals = [None] * at_once
            for di in range(3):
                for k, (i, j, xa, ya) in enumerate(places):
                    xb = jnp.concatenate([px[i + di, pl.ds(j + dj, 1), :] for dj in range(3)], 1)
                    yb = jnp.concatenate([py[i + di, pl.ds(j + dj, 1), :] for dj in range(3)], 1)
                    weights = []
                    for a in range(0, slots, CHUNK):
                        dx = xa[a : a + CHUNK] - xb
                        dy = ya[a : a + CHUNK] - yb
                        d2 = jnp.maximum(dx * dx + dy * dy, 1e-30)
                        s = jnp.maximum(1.0 - d2 * lax.rsqrt(d2), 0.0)
                        w = s * s * s
                        high = w.astype(jnp.bfloat16)
                        low_part = (w - high.astype(jnp.float32)).astype(jnp.bfloat16)
                        weights.append(jnp.concatenate([high, low_part], axis=1))
                    q = feats[i + di, :, pl.ds(pl.multiple_of(j * slots, slots), 3 * slots)]
                    part = lax.dot_general(
                        jnp.concatenate(weights, axis=0),
                        jnp.concatenate([q, q], axis=1),
                        (((1,), (1,)), ((), ())),
                        preferred_element_type=jnp.float32,
                    )
                    totals[k] = part if di == 0 else totals[k] + part
            for k, (i, j, xa, ya) in enumerate(places):
                sums[i * rows + j] = totals[k].T
            return carry

        lax.fori_loop(0, count // at_once, some_bins, 0)

    def inner(n):
        return 1 + n // (rows - 2), 1 + n % (rows - 2)

    def sides(n):
        return (n // rows) * (cols - 1), n % rows

    def ends(n):
        return 1 + n // 2, (n % 2) * (rows - 1)

    def rates(i):
        def take(f):
            block = pl.ds(i * rows, rows)
            if f == 0:
                return sums[block, 0, :]
            first = 1 + 3 * (f - 1)
            return sums[block, first, :] + (sums[block, first + 1, :] + sums[block, first + 2, :])

        s1, sx, sy, sp, spx, spy, su, sv, sc = [take(f) for f in range(FEATURES)]
        own = pl.ds(1, rows)
        x, y = px[i + 1, own, :], py[i + 1, own, :]
        u, v = padded[2, i + 1, own, :], padded[3, i + 1, own, :]
        p = SOUND_SQ * (padded[4, i + 1, own, :] - 1.0)
        away_x, away_y = x * s1 - sx, y * s1 - sy
        force_x = FORCE_SCALE * (p * away_x + (x * sp - spx))
        force_y = FORCE_SCALE * (p * away_y + (y * sp - spy)) - GRAVITY
        compress = -FORCE_SCALE * ((u * away_x + v * away_y) - (x * su + y * sv) + sc)
        return force_x, force_y, compress

    def one_pass(source, stage):
        copies = halo(source, stage)
        fill_rims(source, stage)
        if stage == 0:
            pl.semaphore_wait(
                barrier,
                len(along) + len(across)
                + 2 * has_above.astype(jnp.int32) + 2 * has_below.astype(jnp.int32),
            )
        send(copies)
        padded[:, 1 : cols + 1, 1 : rows + 1, :] = source[...]
        build(1, cols + 1)
        sum_bins((cols - 2) * (rows - 2), inner)
        receive(copies, stage)
        build(0, pcols)
        sum_bins(2 * rows, sides)
        sum_bins(2 * (cols - 2), ends)

    half_step = 0.5 * TIME_STEP
    staged[...] = jnp.zeros_like(staged)
    padded[...] = jnp.zeros_like(padded)

    one_pass(fields, 0)
    for i in range(cols):
        force_x, force_y, compress = rates(i)
        x, y, u, v, rho = [fields[k, i] for k in range(5)]
        values = (
            x + half_step * u,
            y + half_step * v,
            u + half_step * force_x,
            v + half_step * force_y,
            rho + half_step * compress,
        )
        for k, value in enumerate(values):
            predicted[k, i] = jnp.where(x > 0.5 * FAR_SHIFT, value, 0.0)

    one_pass(predicted, 1)
    lowest = None
    for i in range(cols):
        force_x, force_y, compress = rates(i)
        x, y, u, v, rho = [fields[k, i] for k in range(5)]
        occupied = x > 0.5 * FAR_SHIFT
        new_u, new_v = u + TIME_STEP * force_x, v + TIME_STEP * force_y
        new_rho = rho + TIME_STEP * compress
        values = (
            x + half_step * (u + new_u) - FAR_SHIFT,
            y + half_step * (v + new_v) - FAR_SHIFT,
            new_u,
            new_v,
            new_rho,
        )
        for k, value in enumerate(values):
            out[k, i] = jnp.where(occupied, value, 0.0)
        least = jnp.min(jnp.where(occupied, new_rho, EMPTY_DENSITY), axis=0, keepdims=True)
        lowest = least if lowest is None else jnp.minimum(lowest, least)

    def gather(src, land, first, places):
        copies = [
            remote(src, land.at[k], low_send.at[first + k], low_recv.at[first + k], place)
            for k, place in enumerate(places)
        ]
        for copy in copies:
            copy.start()
        for copy in copies:
            copy.wait()
        least = src[...]
        for k in range(len(places)):
            least = jnp.minimum(least, land[k])
        return least

    mine[0] = jnp.broadcast_to(lowest, mine.shape[1:])
    mine[1] = gather(mine.at[0], low_chan, 0, along)
    least = gather(mine.at[1], low_cross, len(along), across)
    low[...] = jnp.broadcast_to(jnp.min(least, keepdims=True), low.shape)


def whole_step(fields):
    count, cols, rows, slots = fields.shape
    pcols, prows = cols + 2, rows + 2
    sublanes = -(-cols // 8) * 8
    chans, crosses = lax.axis_size("chan"), lax.axis_size("cross")
    peers = chans + crosses - 2
    vmem = pl.BlockSpec(memory_space=pltpu.VMEM)
    pairs = 2 * 9 * cols * rows * slots * slots
    held = [
        (count, pcols, prows, slots),
        (count, cols, rows, slots),
        (2, count, sublanes, slots),
        (2, count, sublanes, slots),
        (2, 2, count, rows, slots),
        (2, 6, count, sublanes, slots),
        (pcols, prows, slots),
        (pcols, prows, slots),
        (prows, QROWS, slots),
    ]
    return pl.pallas_call(
        step_kernel,
        out_shape=[
            jax.ShapeDtypeStruct(fields.shape, jnp.float32),
            jax.ShapeDtypeStruct((8, slots), jnp.float32),
        ],
        in_specs=[vmem],
        out_specs=[vmem, vmem],
        scratch_shapes=[pltpu.VMEM(shape, jnp.float32) for shape in held]
        + [
            pltpu.VMEM((pcols, QROWS, prows * slots), jnp.bfloat16),
            pltpu.VMEM((cols * rows, QROWS, slots), jnp.float32),
            pltpu.VMEM((2, 8, slots), jnp.float32),
            pltpu.VMEM((chans - 1, 8, slots), jnp.float32),
            pltpu.VMEM((crosses - 1, 8, slots), jnp.float32),
            pltpu.SemaphoreType.DMA((2, 8)),
            pltpu.SemaphoreType.DMA((2, 8)),
            pltpu.SemaphoreType.DMA((peers,)),
            pltpu.SemaphoreType.DMA((peers,)),
        ],
        compiler_params=pltpu.CompilerParams(
            collective_id=0, has_side_effects=True, vmem_limit_bytes=32 * 1024 * 1024
        ),
        cost_estimate=pl.CostEstimate(
            flops=pairs * 40, bytes_accessed=4 * 1024 * 1024, transcendentals=pairs
        ),
    )(fields)


def body(positions, velocity, density, counts):
    slot_index = jnp.arange(positions.shape[-1], dtype=jnp.int32)
    occupied = slot_index[None, None, :] < counts[:, :, None]
    fields = jnp.concatenate([positions + FAR_SHIFT, velocity, density[None]], axis=0)
    fields = jnp.where(occupied[None], fields, 0.0)
    new_fields, low = whole_step(fields)
    return (new_fields, low[0, 0])


def solution(mesh):
    return jax.shard_map(
        body,
        mesh=mesh,
        in_specs=(
            P(None, "chan", "cross", None),
            P(None, "chan", "cross", None),
            P("chan", "cross", None),
            P("chan", "cross"),
        ),
        out_specs=(P(None, "chan", "cross", None), P()),
        check_vma=False,
    )
```

time: 138 us -> 76.2 us (0.55)
  blocking collectives: 39.5 us -> 0 us
  starting transfers between devices: 14.4 us -> 0 us
  waiting for transfers between devices: 7.02 us -> 0 us
    pmin x1 -> x0, blocking collectives: 39.5 us -> none  [body(): lowest = lax.pmin(jnp.min(low), ('chan', 'cross'))]
    ppermute x8 -> x0, starting transfers between devices: 14.4 us -> none  [the longest x4 10.2 us: exchange(): after = lax.ppermute(leading, axis, down)]
    ppermute x8 -> x0, waiting for transfers between devices: 7.02 us -> none  [the longest x4 6.88 us: exchange(): before = lax.ppermute(last, axis, up)]
    pallas_call x2 -> x1, Pallas kernels: 73.1 us -> 72.5 us  [whole_step(): pl.pallas_call(step_kernel, out_shape=[jax.ShapeDtypeStruct(fields.shape,...]
  transfers between devices with their start and end apart: 8 -> 0, of which waited for: 6 -> 0; matrix products, arithmetic and copies ran while one was open for 0% -> 0% of each run, Pallas kernels for 0% -> 0%
where the time goes in v3:
time: 76.2 us; the launch traced here: 76 us
  Pallas kernels  72.5 us (95%)
  other arithmetic  1.65 us (2%)
  local copies, waits for them, and re-layouts  1.19 us (2%)
    pallas_call x1, Pallas kernels, whole_step(): pl.pallas_call(step_kernel, out_shape=[jax.ShapeDtypeStruct(fields.shape,...  72.5 us

profile of v3, /device:TPU:0, one launch (start us, length us, event | category | flops | bytes accessed | tf_op | source)
XLA Modules:
  0.0 76.0 jit_solution(17178123891518881702)
XLA Ops:
  0.6 0.8 iota_compare_fusion
  1.4 0.0 copy-start
  1.4 0.0 copy-start.1
  1.4 0.9 %broadcast_add_fusion = f32[2,4,16,128]{3,2,1,0:T(8,128)S(1)} fusion(f32[2,4,16,128]{3,2,1,0:T(8,128)} %param.4), kind=kLoop, calls=%fused_computation.1 | loop fusion | flops 16384 | bytes 131072 | tf_op jit(solution)/shard_map/add | solution.py:339
  2.3 0.0 copy-done
  2.3 0.0 copy-done.1
  2.3 72.5 %shard_map.59 = (f32[5,4,16,128]{3,2,1,0:T(8,128)S(1)}, f32[8,128]{1,0:T(8,128)S(1)}) custom-call(f32[5,4,16,128]{3,2,1,0:T(8,128)S(1)} %maximum_select_fusion.fields), custom_call_target="tpu_custom_call" | custom-call | flops 754974720 | bytes 4194304 | tf_op jit(solution)/shard_map/pallas_call | solution.py:307
  74.8 0.5 slice.3
  75.3 0.7 copy.7
  (1 shorter events, 0.0 us)
Async XLA Ops:
  1.4 0.9 %copy-start = (f32[2,4,16,128]{3,2,1,0:T(8,128)S(1)}, f32[2,4,16,128]{3,2,1,0:T(8,128)}, u32[]{:S(2)}) copy-start(f32[2,4,16,128]{3,2,1,0:T(8,128)} %param.5) | copy-start | bytes 196612
  1.4 0.9 %copy-start.1 = (f32[4,16,128]{2,1,0:T(8,128)S(1)}, f32[4,16,128]{2,1,0:T(8,128)}, u32[]{:S(2)}) copy-start(f32[4,16,128]{2,1,0:T(8,128)} %param.6) | copy-start | bytes 98308
